TPU v7x, 32 devices: a whole 2x2x4 slice. The times are simulated.
32 devices in a mesh: groups: 2 (over y), sector: 4 (over z), op: 4 (over x, core).
Axes of the slice: x: 2, y: 2, z: 4, core: 2. Of those that a mesh axis runs over, the one named last changes fastest.
Arguments:
- psi: float32 [32, 256, 256], P(('groups', 'sector')), parts along dimension 0, may hold values from -6 to 6
- left_env: float32 [40, 32, 256, 256], P('op', ('groups', 'sector')), parts along dimension 1, may hold values from -0.375 to 0.375
- right_env: float32 [40, 32, 256, 256], P('op', ('groups', 'sector')), parts along dimension 1, may hold values from -0.375 to 0.375
- source: int32 [40, 32], P(None, 'groups'), parts along dimension 1, may hold values from 0 to 15, as said below
- coef_index: int32 [40, 32], P('op', ('groups', 'sector')), parts along dimension 1, may hold values from 0 to 23
- coef_table: float32 [24], replicated, may hold values from 0.1 to 0.3
Outputs:
- h_psi: float32 [32, 256, 256], P(('groups', 'sector'), 'op'), parts along dimension 0
There are 2 independent parts, one for each index of `groups`. A program takes and returns all parts, laid end to end along the dimension named above; an argument that names none is the same for every part. Nothing has to cross between parts.
Inputs may be any that keep to these rules, and one draw needn't show every extreme that they name: For each block of 10 consecutive terms and each block of 4 consecutive target sectors, at most 10 of these pairs read a source sector from any one block of 4 consecutive sectors, and some such block is read exactly 10 times.
All inputs are finite; a program needn't handle non-finite values.
Results may differ from a plain program's by a relative error of at most 0.0003.
Values sent between devices are 32-bit elements; how exact they have to be, the bound alone decides.
A program may use at most 128 MiB of HBM per device.

v0:
```python
import jax
import jax.numpy as jnp
from jax import lax
from jax.sharding import PartitionSpec as P


def on_device(psi, left_env, right_env, source, coef_index, coef_table):
    sec_dev = psi.shape[0]
    block = psi.shape[1]
    term_dev = left_env.shape[0]
    my_sec = lax.axis_index("sector")
    my_op = lax.axis_index("op")
    own_src = lax.dynamic_slice(source, (my_op * term_dev, my_sec * sec_dev), (term_dev, sec_dev))
    everything = lax.all_gather(psi, "sector", axis=0, tiled=True)
    blocks = jnp.take(everything, own_src.reshape(-1), axis=0)
    blocks = blocks.reshape(term_dev, sec_dev, block, block)
    levels = jnp.arange(coef_table.shape[0], dtype=jnp.int32)
    coef = jnp.sum(
        jnp.where(coef_index[..., None] == levels, coef_table, jnp.zeros_like(coef_table)), axis=-1
    )
    partial_value = (
        jnp.einsum("wsab,wsbc->wsac", blocks, right_env, precision=lax.Precision.HIGHEST)
        * coef[:, :, None, None]
    )
    share = lax.psum_scatter(
        jnp.einsum("wsrk,wskc->rsc", left_env, partial_value, precision=lax.Precision.HIGHEST),
        "op",
        scatter_dimension=0,
        tiled=True,
    )
    return share.transpose(1, 0, 2)


def solution(mesh):
    return jax.shard_map(
        on_device,
        mesh=mesh,
        in_specs=(
            P(("groups", "sector"), None, None),
            P("op", ("groups", "sector"), None, None),
            P("op", ("groups", "sector"), None, None),
            P(None, "groups"),
            P("op", ("groups", "sector")),
            P(),
        ),
        out_specs=P(("groups", "sector"), "op", None),
        check_vma=False,
    )
```

profile of v0, /device:TPU:0, one launch (start us, length us, event | category | flops | bytes accessed | tf_op | source)
XLA Modules:
  0.0 187.4 jit_solution(6010511600737618949)
XLA Ops:
  6.5 0.0 all-gather.2.cloned.1.call-start
  6.5 0.7 all-gather.2.cloned.1.call-update
  7.3 0.0 all-reduce.3.cloned.1.call-start
  7.3 0.8 compare_and_fusion
  8.1 0.1 copy.25
  8.2 0.1 reshape.42
  8.3 0.8 copy.28
  9.0 0.8 select_reduce_fusion
  9.8 0.1 copy.29
  9.9 82.5 %all-gather.2.cloned.1.call-done = f32[16,256,256]{2,1,0:T(8,128)} async-done(((f32[4,256,256]{2,1,0:T(8,128)}), f32[16,256,256]{2,1,0:T(8,128)}) %all-gather.2.cloned.1.call-update) | async-done | bytes 4194320 | tf_op jit(solution)/shard_map/all_gather | solution.py:14
  92.4 9.2 %gather_fusion = f32[40,256,256]{2,1,0:T(8,128)} fusion(f32[16,256,256]{2,1,0:T(8,128)} %all-gather.2.cloned.1.call-done, s32[1024]{0:T(1024)S(1)} %pad_clamp_fusion), kind=kCustom, calls=%fused_computation | custom fusion | bytes 20971680 | tf_op jit(solution)/shard_map/jit(_take)/gather | solution.py:15
  101.6 19.8 %fusion.2 = f32[10,4,256,256]{3,2,0,1:T(8,128)} fusion(f32[10,4,256,256]{3,2,1,0:T(8,128)} %param.8, f32[10,4,256,256]{3,2,1,0:T(8,128)} %bitcast.11, pred[10,4]{0,1:T(4,128)(4,1)S(1)} %get-tuple-element.5), kind=kOutput, calls=%fused_computation.3 | convolution fusion | flops 8055685120 | bytes 31457320 | tf_op jit(solution)/shard_map/wsab,wsbc->wsac/dot_general | solution.py:22
  121.4 0.0 copy-start
  121.4 21.3 %fusion.8 = f32[256,4,256]{0,2,1:T(8,128)S(1)} fusion(f32[10,4,256,256]{3,2,1,0:T(8,128)} %param.7, f32[10,4,256,256]{3,2,0,1:T(8,128)} %fusion.2, f32[10,4]{0,1:T(4,128)S(1)} %copy.29), kind=kOutput, calls=%fused_computation.10 | convolution fusion | flops 8055685120 | bytes 22020256 | tf_op jit(solution)/shard_map/wsrk,wskc->rsc/dot_general | solution.py:26
  142.7 1.4 copy.32
  144.0 0.0 all-reduce.3.cloned.1.call-update
  144.0 0.0 copy-done
  144.1 0.6 dynamic-slice
  145.3 33.6 %all-reduce.3.cloned.1.call-done = f32[256,4,256]{2,1,0:T(4,128)} async-done(((f32[256,4,256]{2,1,0:T(4,128)}), f32[256,4,256]{2,1,0:T(4,128)}) %all-reduce.3.cloned.1.call-update) | async-done | bytes 1048592
  178.8 1.0 dynamic-slice_bitcast_fusion
  179.8 0.8 copy.33
  (2 shorter events, 0.0 us)
Async XLA Ops:
  6.5 85.9 %all-gather.2.cloned.1.call-start = ((), (), s32[]{:S(2)}) async-start(), calls=%async_computation | async-start | bytes 5242880 | tf_op jit(solution)/shard_map/all_gather | solution.py:14
  7.3 171.6 %all-reduce.3.cloned.1.call-start = ((), (), s32[]{:S(2)}) async-start(), calls=%async_computation.1 | async-start | bytes 2097152
  121.4 22.7 %copy-start = (u32[32]{0:T(128)S(1)}, u32[32]{0:T(128)}, u32[]{:S(2)}) copy-start(u32[32]{0:T(128)} %constant.40) | copy-start | bytes 388
Sparse Core Ops, SparseCore 0:
  8.9 83.4 all-gather.1
  144.2 34.6 all-reduce.2
where the time goes:
time: 188 us; the launch traced here: 187 us
  waiting for transfers between devices  117 us (62%)
  matrix products  41 us (22%)
  between operations  14.1 us (8%)
  local copies, waits for them, and re-layouts  13.9 us (7%)
    all_gather x1, waiting for transfers between devices, on_device(): everything = lax.all_gather(psi, 'sector', axis=0, tiled=True)  82.5 us
    unnamed x3, waiting for transfers between devices  34.3 us
    dot_general x1, matrix products, on_device(): jnp.einsum('wsrk,wskc->rsc', left_env, partial_value, precision=lax.Preci...  21.3 us
    dot_general x1, matrix products, on_device(): jnp.einsum('wsab,wsbc->wsac', blocks, right_env, precision=lax.Precision....  19.8 us
    gather x1, local copies, waits for them, and re-layouts, on_device(): blocks = jnp.take(everything, own_src.reshape(-1), axis=0)  9.19 us
  transfers between devices with their start and end apart: 2, of which 2 were waited for; matrix products, arithmetic and copies ran while one was open for 2% of the time, Pallas kernels for 0%

commit v1 on v0

v1 whole, which is shorter than its diff:
```python
import functools

import jax
import jax.numpy as jnp
from jax import lax
from jax.experimental import pallas as pl
from jax.experimental.pallas import tpu as pltpu
from jax.sharding import PartitionSpec as P

F32 = jnp.float32
BF16 = jnp.bfloat16
MESH = pl.DeviceIdType.MESH


def split(value):
    high = value.astype(BF16)
    return high, (value - high.astype(F32)).astype(BF16)


def dot3(a_hi, a_lo, b_hi, b_lo):
    dot = functools.partial(jnp.dot, preferred_element_type=F32)
    return dot(a_hi, b_hi) + dot(a_hi, b_lo) + dot(a_lo, b_hi)


def kernel(nz, nx, cap, parts, order_ref, inner_ref, coef_ref, slot_ref, psi_ref, left_ref, right_ref, out_ref,
           psi_all, left, right, cur_hi, cur_lo, par_hi, par_lo, h, first, summed, second,
           load_sem, recv_sem, z_sem, x_sem, c_sem, r1_send, r1_recv, r2_send, r2_recv):
    sec = psi_ref.shape[0]
    block = psi_ref.shape[1]
    terms = left_ref.shape[0]
    nop = 2 * nx
    rows = block // nop
    part = sec // parts
    z = lax.axis_index("sector")
    o = lax.axis_index("op")
    x = o // 2
    c = lax.rem(o, 2)
    mate = 2 * x + 1 - c

    load_psi = pltpu.make_async_copy(psi_ref, psi_all.at[z], load_sem.at[0])
    load_right = pltpu.make_async_copy(right_ref, right, load_sem.at[1])
    load_left = pltpu.make_async_copy(left_ref, left, load_sem.at[2])
    load_psi.start()
    load_right.start()
    load_left.start()

    def other(step):
        return lax.rem(x + step, nx)

    barrier = pltpu.get_barrier_semaphore()

    @pl.when(z > 0)
    def _():
        pl.semaphore_signal(barrier, inc=1, device_id={"sector": z - 1}, device_id_type=MESH)

    @pl.when(z < nz - 1)
    def _():
        pl.semaphore_signal(barrier, inc=1, device_id={"sector": z + 1}, device_id_type=MESH)

    pl.semaphore_signal(barrier, inc=1, device_id={"op": mate}, device_id_type=MESH)
    for step in range(1, nx):
        pl.semaphore_signal(barrier, inc=1, device_id={"op": 2 * other(step) + c}, device_id_type=MESH)

    inside = jnp.logical_and(z > 0, z < nz - 1)

    @pl.when(inside)
    def _():
        pl.semaphore_wait(barrier, nx + 2)

    @pl.when(jnp.logical_not(inside))
    def _():
        pl.semaphore_wait(barrier, nx + 1)

    def piece(k, i, q):
        return psi_all.at[k, pl.ds(i * part, part), pl.ds(pl.multiple_of(q * rows, rows), rows), :]

    def send(k, i, q, sem, device):
        return pltpu.make_async_remote_copy(
            src_ref=piece(k, i, q), dst_ref=piece(k, i, q), send_sem=sem, recv_sem=recv_sem.at[k, i, q],
            device_id=device, device_id_type=MESH)

    def z_copy(k, i, way):
        return send(k, i, o, z_sem.at[(way + 1) // 2, k, i], {"sector": z + way})

    def x_copy(k, i, step):
        return send(k, i, o, x_sem.at[k, i, step], {"op": 2 * other(step) + c})

    def c_copy(k, i, xq):
        return send(k, i, 2 * xq + c, c_sem.at[k, i, xq], {"op": mate})

    def arrived(k, i, q):
        send(k, i, q, z_sem.at[0, k, i], {"op": mate}).wait_recv()

    load_psi.wait()
    for i in range(parts):
        for way in (-1, 1):
            @pl.when(jnp.logical_and(z + way >= 0, z + way < nz))
            def _():
                z_copy(z, i, way).start()

    def products(k):
        def halve(s, carry):
            cur_hi[s], cur_lo[s] = split(psi_all[k, s])
            return carry
        lax.fori_loop(0, sec, halve, 0)

        def pair(j, carry):
            at = k * cap + j
            p = order_ref[at]
            s = inner_ref[at]
            r_hi, r_lo = split(right[p // sec, lax.rem(p, sec)])
            value = dot3(cur_hi[s], cur_lo[s], r_hi, r_lo) * coef_ref[at]
            par_hi[at], par_lo[at] = split(value)
            return carry
        lax.fori_loop(0, cap, pair, 0)

    load_right.wait()
    products(z)

    def both(d, body):
        for side in (-1, 1):
            k = z + side * d
            @pl.when(jnp.logical_and(d >= 1, jnp.logical_and(d < nz, jnp.logical_and(k >= 0, k < nz))))
            def _():
                body(k, side)

    def take_z(i):
        def body(k, side):
            arrived(k, i, o)
            ahead = z - side

            @pl.when(jnp.logical_and(ahead >= 0, ahead < nz))
            def _():
                z_copy(k, i, -side).start()
            for step in range(1, nx):
                x_copy(k, i, step).start()
            c_copy(k, i, x).start()
        return body

    def take_x(i):
        def body(k, side):
            for step in range(1, nx):
                arrived(k, i, 2 * other(step) + c)
                c_copy(k, i, other(step)).start()
        return body

    def take_all(k, side):
        for i in range(parts):
            for xq in range(nx):
                arrived(k, i, 2 * xq + 1 - c)
        products(k)

    def stage(d, carry):
        for i in range(parts):
            both(d, take_z(i))
            both(d - 1, take_x(i))
        both(d - 2, take_all)
        return carry
    lax.fori_loop(1, nz + 2, stage, 0)

    load_left.wait()

    def mine(t, xq, core):
        return h.at[t, pl.ds(pl.multiple_of((2 * xq + core) * rows, rows), rows), :]

    def r1_copy(t, xq):
        return pltpu.make_async_remote_copy(
            src_ref=mine(t, xq, 1 - c), dst_ref=first.at[t, xq], send_sem=r1_send.at[t, xq],
            recv_sem=r1_recv.at[t, xq], device_id={"op": mate}, device_id_type=MESH)

    def r2_copy(t, step):
        return pltpu.make_async_remote_copy(
            src_ref=summed.at[t, other(step)], dst_ref=second.at[t, step], send_sem=r2_send.at[t, step],
            recv_sem=r2_recv.at[t, step], device_id={"op": 2 * other(step) + c}, device_id_type=MESH)

    def target(t, carry):
        @pl.when(t < sec)
        def _():
            def term(w, carry):
                slot = slot_ref[w * sec + t]
                l_hi, l_lo = split(left[w, t])
                value = dot3(l_hi, l_lo, par_hi[slot], par_lo[slot])

                @pl.when(w == 0)
                def _():
                    h[t] = value

                @pl.when(w > 0)
                def _():
                    h[t] = h[t] + value
                return carry
            lax.fori_loop(0, terms, term, 0)
            for xq in range(nx):
                r1_copy(t, xq).start()

        @pl.when(t >= 1)
        def _():
            b = t - 1
            for xq in range(nx):
                r1_copy(b, xq).wait_recv()
                summed[b, xq] = mine(b, xq, c)[...] + first[b, xq]
            for step in range(1, nx):
                r2_copy(b, step).start()
        return carry
    lax.fori_loop(0, sec + 1, target, 0)

    def finish(t, carry):
        total = summed[t, x]
        for step in range(1, nx):
            r2_copy(t, step).wait_recv()
            total = total + second[t, step]
        out_ref[t] = total
        for step in range(1, nx):
            r2_copy(t, step).wait_send()
        for xq in range(nx):
            r1_copy(t, xq).wait_send()
        return carry
    lax.fori_loop(0, sec, finish, 0)

    for i in range(parts):
        for way in (-1, 1):
            @pl.when(jnp.logical_and(z + way >= 0, z + way < nz))
            def _():
                z_copy(z, i, way).wait_send()

    def drain(i):
        def body(k, side):
            ahead = z - side

            @pl.when(jnp.logical_and(ahead >= 0, ahead < nz))
            def _():
                z_copy(k, i, -side).wait_send()
            for step in range(1, nx):
                x_copy(k, i, step).wait_send()
            for xq in range(nx):
                c_copy(k, i, xq).wait_send()
        return body

    def last(d, carry):
        for i in range(parts):
            both(d, drain(i))
        return carry
    lax.fori_loop(1, nz, last, 0)


def on_device(nz, nop, psi, left_env, right_env, source, coef_index, coef_table):
    sec, block, _ = psi.shape
    terms = left_env.shape[0]
    pairs = terms * sec
    cap = -(-pairs // nz)
    slots = cap * nz
    nx = nop // 2
    rows = block // nop
    parts = 2
    my_sec = lax.axis_index("sector")
    my_op = lax.axis_index("op")
    src = lax.dynamic_slice(source, (my_op * terms, my_sec * sec), (terms, sec)).reshape(-1)
    owner = src // sec
    index = jnp.arange(pairs, dtype=jnp.int32)
    earlier = (owner[None, :] == owner[:, None]) & (index[None, :] < index[:, None])
    slot = owner * cap + jnp.sum(earlier, axis=1, dtype=jnp.int32)
    hit = slot[None, :] == jnp.arange(slots, dtype=jnp.int32)[:, None]
    order = jnp.sum(jnp.where(hit, index[None, :], 0), axis=1, dtype=jnp.int32)
    inner = jnp.sum(jnp.where(hit, (src % sec)[None, :], 0), axis=1, dtype=jnp.int32)
    levels = jnp.arange(coef_table.shape[0], dtype=jnp.int32)
    coef = jnp.sum(
        jnp.where(coef_index.reshape(-1)[:, None] == levels, coef_table, jnp.zeros_like(coef_table)), axis=-1
    )
    coef = jnp.sum(jnp.where(hit, coef[None, :], 0.0), axis=1)
    dma = pltpu.SemaphoreType.DMA
    smem = pl.BlockSpec(memory_space=pltpu.SMEM)
    hbm = pl.BlockSpec(memory_space=pl.ANY)
    return pl.pallas_call(
        functools.partial(kernel, nz, nx, cap, parts),
        out_shape=jax.ShapeDtypeStruct((sec, rows, block), F32),
        in_specs=[smem] * 4 + [hbm] * 3,
        out_specs=pl.BlockSpec(memory_space=pltpu.VMEM),
        scratch_shapes=[
            pltpu.VMEM((nz, sec, block, block), F32),
            pltpu.VMEM((terms, sec, block, block), F32),
            pltpu.VMEM((terms, sec, block, block), F32),
            pltpu.VMEM((sec, block, block), BF16),
            pltpu.VMEM((sec, block, block), BF16),
            pltpu.VMEM((slots, block, block), BF16),
            pltpu.VMEM((slots, block, block), BF16),
            pltpu.VMEM((sec, block, block), F32),
            pltpu.VMEM((sec, nx, rows, block), F32),
            pltpu.VMEM((sec, nx, rows, block), F32),
            pltpu.VMEM((sec, nx, rows, block), F32),
            dma((3,)),
            dma((nz, parts, nop)),
            dma((2, nz, parts)),
            dma((nz, parts, nx)),
            dma((nz, parts, nx)),
            dma((sec, nx)),
            dma((sec, nx)),
            dma((sec, nx)),
            dma((sec, nx)),
        ],
        compiler_params=pltpu.CompilerParams(
            collective_id=0, has_side_effects=True, vmem_limit_bytes=56 * 1024 * 1024
        ),
        cost_estimate=pl.CostEstimate(
            flops=12 * pairs * block ** 3, bytes_accessed=8 * pairs * block * block, transcendentals=0
        ),
    )(order, inner, coef, slot, psi, left_env, right_env)


def solution(mesh):
    return jax.shard_map(
        functools.partial(on_device, mesh.shape["sector"], mesh.shape["op"]),
        mesh=mesh,
        in_specs=(
            P(("groups", "sector"), None, None),
            P("op", ("groups", "sector"), None, None),
            P("op", ("groups", "sector"), None, None),
            P(None, "groups"),
            P("op", ("groups", "sector")),
            P(),
        ),
        out_specs=P(("groups", "sector"), "op", None),
        check_vma=False,
    )
```

time: 188 us -> 60.9 us (0.32)
  the two profiles are of different devices: /device:TPU:0 before, /device:TPU:21 now
where the time goes in v1:
time: 60.9 us; the launch traced here: 60.6 us
  Pallas kernels  54.9 us (90%)
  local copies, waits for them, and re-layouts  3.47 us (6%)
  other arithmetic  2.29 us (4%)
    pallas_call x1, Pallas kernels, on_device(): pl.pallas_call(functools.partial(kernel, nz, nx, cap, parts), out_shape=j...  54.9 us
    unnamed x4, local copies, waits for them, and re-layouts  2.45 us

profile of v1, /device:TPU:21, one launch (start us, length us, event | category | flops | bytes accessed | tf_op | source)
XLA Modules:
  0.0 60.6 jit_solution(12463061632580186935)
XLA Ops:
  0.0 0.8 %dynamic_slice.3 = s32[10,4]{0,1:T(4,128)S(1)} dynamic-slice(s32[40,16]{0,1:T(8,128)} %param.9, s32[]{:T(128)S(6)} %select_n.48, s32[]{:T(128)S(6)} %select_n.49), dynamic_slice_sizes={10,4} | dynamic-slice | bytes 324 | tf_op jit(solution)/shard_map/dynamic_slice | solution.py:257
  0.8 0.1 copy.11
  0.9 0.1 reshape.95
  1.0 0.2 convert_reduce_fusion
  1.1 0.0 copy-start
  1.2 0.7 %select_reduce_fusion.1 = (s32[40]{0:T(128)}, s32[40]{0:T(128)}) fusion(s32[40]{0:T(128)S(1)} %get-tuple-element.8, s32[40]{0:T(128)S(1)} %multiply_add_fusion.slot_ref), kind=kLoop, calls=%fused_computation.1 | loop fusion | flops 7920 | bytes 640 | tf_op jit(solution)/shard_map/reduce_sum | solution.py:264
  1.9 0.8 %copy.12 = s32[10,4]{1,0:T(8,128)S(1)} copy(s32[10,4]{0,1:T(4,128)} %param.10) | data formatting | bytes 320 | tf_op args[4]
  2.6 0.1 eq.46
  2.7 0.7 %select_reduce_fusion.3 = f32[40]{0:T(128)S(1)} fusion(f32[24]{0:T(128)} %param.11, s32[40]{0:T(128)S(1)} %eq.46), kind=kLoop, calls=%fused_computation.7 | loop fusion | flops 2840 | bytes 416 | tf_op jit(solution)/shard_map/reduce_sum | solution.py:266
  3.4 0.7 %select_reduce_fusion.coef_ref = f32[40]{0:T(128)} fusion(f32[40]{0:T(128)S(1)} %select_reduce_fusion.3, s32[40]{0:T(128)S(1)} %multiply_add_fusion.slot_ref), kind=kLoop, calls=%fused_computation | loop fusion | flops 4760 | bytes 480 | tf_op jit(solution)/shard_map/reduce_sum | solution.py:269
  4.1 0.0 copy-done
  4.1 54.9 %shard_map.64 = f32[4,64,256]{2,1,0:T(8,128)} custom-call(s32[40]{0:T(128)} %get-tuple-element.6.order_ref, s32[40]{0:T(128)} %get-tuple-element.5.inner_ref, f32[40]{0:T(128)} %select_reduce_fusion.coef_ref, s32[40]{0:T(128)} %copy-done, f32[4,256,256]{2,1,0:T(8,128)} %psi_ref.1, f32[10,4,256,256]{3,2,1,0:T(8,128)} %left_ref.1, f32[10,4,256,256]{3,2,1,0:T(8,128)} %right_ref.1), custom_call_target="tpu_custom_call" | custom-call | flops 8053063680 | bytes 20971520 | tf_op jit(solution)/shard_map/pallas_call | solution.py:273
  59.0 1.7 %copy.14 = f32[4,64,256]{2,1,0:T(8,128)} copy(f32[4,64,256]{2,1,0:T(8,128)} %shard_map.64) | data formatting | bytes 524288
  (2 shorter events, 0.0 us)
Async XLA Ops:
  1.1 3.0 %copy-start = (s32[40]{0:T(128)}, s32[40]{0:T(128)S(1)}, u32[]{:S(2)}) copy-start(s32[40]{0:T(128)S(1)} %multiply_add_fusion.slot_ref) | copy-start | bytes 484

commit v2 on v1

--- a/solution.py
+++ b/solution.py
@@ -22,13 +22,14 @@
     return dot(a_hi, b_hi) + dot(a_hi, b_lo) + dot(a_lo, b_hi)
 
 
-def kernel(nz, nx, cap, parts, order_ref, inner_ref, coef_ref, slot_ref, psi_ref, left_ref, right_ref, out_ref,
-           psi_all, left, right, cur_hi, cur_lo, par_hi, par_lo, h, first, summed, second,
+def kernel(nz, nx, cap, parts, source_ref, index_ref, table_ref, psi_ref, left_ref, right_ref, out_ref,
+           after, rank, reads, psi_all, left, right, cur_hi, cur_lo, contrib, h, first, summed, second,
            load_sem, recv_sem, z_sem, x_sem, c_sem, r1_send, r1_recv, r2_send, r2_recv):
     sec = psi_ref.shape[0]
     block = psi_ref.shape[1]
     terms = left_ref.shape[0]
     nop = 2 * nx
+    pairs = terms * sec
     rows = block // nop
     part = sec // parts
     z = lax.axis_index("sector")
@@ -98,24 +99,54 @@
             def _():
                 z_copy(z, i, way).start()
 
-    def products(k):
+    def source_of(p):
+        return source_ref[o * terms + lax.div(p, sec), z * sec + lax.rem(p, sec)]
+
+    def clear(p, carry):
+        rank[p] = 0
+        return carry
+    lax.fori_loop(0, pairs, clear, 0)
+
+    def chain(k):
+        def backward(step, carry):
+            found, count = carry
+            p = pairs - 1 - step
+            hit = lax.div(source_of(p), sec) == k
+            after[p] = found
+            rank[p] = jnp.where(hit, count, rank[p])
+            return jnp.where(hit, p, found), jnp.where(hit, count + 1, count)
+        found, count = lax.fori_loop(0, pairs, backward, (0, 0))
+        reads[k] = count
+        return found
+
+    def slot(p):
+        owner = lax.div(source_of(p), sec)
+        return owner * cap + reads[owner] - 1 - rank[p]
+
+    def ready(k):
         def halve(s, carry):
             cur_hi[s], cur_lo[s] = split(psi_all[k, s])
             return carry
         lax.fori_loop(0, sec, halve, 0)
 
-        def pair(j, carry):
-            at = k * cap + j
-            p = order_ref[at]
-            s = inner_ref[at]
-            r_hi, r_lo = split(right[p // sec, lax.rem(p, sec)])
-            value = dot3(cur_hi[s], cur_lo[s], r_hi, r_lo) * coef_ref[at]
-            par_hi[at], par_lo[at] = split(value)
-            return carry
-        lax.fori_loop(0, cap, pair, 0)
-
+    def products(k, begin, end, start):
+        def pair(j, p):
+            w = lax.div(p, sec)
+            t = lax.rem(p, sec)
+            s = lax.rem(source_of(p), sec)
+            r_hi, r_lo = split(right[w, t])
+            value = dot3(cur_hi[s], cur_lo[s], r_hi, r_lo) * table_ref[index_ref[w, t]]
+            l_hi, l_lo = split(left[w, t])
+            v_hi, v_lo = split(value)
+            contrib[k * cap + j] = dot3(l_hi, l_lo, v_hi, v_lo)
+            return after[p]
+        return lax.fori_loop(begin, end, pair, start)
+
+    ready(z)
+    head = chain(z)
     load_right.wait()
-    products(z)
+    load_left.wait()
+    middle = products(z, 0, cap // 2, head)
 
     def both(d, body):
         for side in (-1, 1):
@@ -148,17 +179,22 @@
         for i in range(parts):
             for xq in range(nx):
                 arrived(k, i, 2 * xq + 1 - c)
-        products(k)
+        ready(k)
+        products(k, 0, cap, chain(k))
 
     def stage(d, carry):
         for i in range(parts):
             both(d, take_z(i))
-            both(d - 1, take_x(i))
-        both(d - 2, take_all)
-        return carry
-    lax.fori_loop(1, nz + 2, stage, 0)
-
-    load_left.wait()
+
+        @pl.when(d == 1)
+        def _():
+            products(z, cap // 2, cap, middle)
+        both(d - 1, take_all)
+        for i in range(parts):
+            both(d, take_x(i))
+        return carry
+    lax.fori_loop(1, nz, stage, 0)
+    both(nz - 1, take_all)
 
     def mine(t, xq, core):
         return h.at[t, pl.ds(pl.multiple_of((2 * xq + core) * rows, rows), rows), :]
@@ -176,20 +212,10 @@
     def target(t, carry):
         @pl.when(t < sec)
         def _():
-            def term(w, carry):
-                slot = slot_ref[w * sec + t]
-                l_hi, l_lo = split(left[w, t])
-                value = dot3(l_hi, l_lo, par_hi[slot], par_lo[slot])
-
-                @pl.when(w == 0)
-                def _():
-                    h[t] = value
-
-                @pl.when(w > 0)
-                def _():
-                    h[t] = h[t] + value
-                return carry
-            lax.fori_loop(0, terms, term, 0)
+            total = contrib[slot(t)]
+            for w in range(1, terms):
+                total = total + contrib[slot(w * sec + t)]
+            h[t] = total
             for xq in range(nx):
                 r1_copy(t, xq).start()
 
@@ -252,37 +278,24 @@
     nx = nop // 2
     rows = block // nop
     parts = 2
-    my_sec = lax.axis_index("sector")
-    my_op = lax.axis_index("op")
-    src = lax.dynamic_slice(source, (my_op * terms, my_sec * sec), (terms, sec)).reshape(-1)
-    owner = src // sec
-    index = jnp.arange(pairs, dtype=jnp.int32)
-    earlier = (owner[None, :] == owner[:, None]) & (index[None, :] < index[:, None])
-    slot = owner * cap + jnp.sum(earlier, axis=1, dtype=jnp.int32)
-    hit = slot[None, :] == jnp.arange(slots, dtype=jnp.int32)[:, None]
-    order = jnp.sum(jnp.where(hit, index[None, :], 0), axis=1, dtype=jnp.int32)
-    inner = jnp.sum(jnp.where(hit, (src % sec)[None, :], 0), axis=1, dtype=jnp.int32)
-    levels = jnp.arange(coef_table.shape[0], dtype=jnp.int32)
-    coef = jnp.sum(
-        jnp.where(coef_index.reshape(-1)[:, None] == levels, coef_table, jnp.zeros_like(coef_table)), axis=-1
-    )
-    coef = jnp.sum(jnp.where(hit, coef[None, :], 0.0), axis=1)
     dma = pltpu.SemaphoreType.DMA
     smem = pl.BlockSpec(memory_space=pltpu.SMEM)
     hbm = pl.BlockSpec(memory_space=pl.ANY)
     return pl.pallas_call(
         functools.partial(kernel, nz, nx, cap, parts),
         out_shape=jax.ShapeDtypeStruct((sec, rows, block), F32),
-        in_specs=[smem] * 4 + [hbm] * 3,
+        in_specs=[smem] * 3 + [hbm] * 3,
         out_specs=pl.BlockSpec(memory_space=pltpu.VMEM),
         scratch_shapes=[
+            pltpu.SMEM((pairs,), jnp.int32),
+            pltpu.SMEM((pairs,), jnp.int32),
+            pltpu.SMEM((nz,), jnp.int32),
             pltpu.VMEM((nz, sec, block, block), F32),
             pltpu.VMEM((terms, sec, block, block), F32),
             pltpu.VMEM((terms, sec, block, block), F32),
             pltpu.VMEM((sec, block, block), BF16),
             pltpu.VMEM((sec, block, block), BF16),
-            pltpu.VMEM((slots, block, block), BF16),
-            pltpu.VMEM((slots, block, block), BF16),
+            pltpu.VMEM((slots, block, block), F32),
             pltpu.VMEM((sec, block, block), F32),
             pltpu.VMEM((sec, nx, rows, block), F32),
             pltpu.VMEM((sec, nx, rows, block), F32),
@@ -303,7 +316,7 @@
         cost_estimate=pl.CostEstimate(
             flops=12 * pairs * block ** 3, bytes_accessed=8 * pairs * block * block, transcendentals=0
         ),
-    )(order, inner, coef, slot, psi, left_env, right_env)
+    )(source, coef_index, coef_table, psi, left_env, right_env)
 
 
 def solution(mesh):

time: 60.9 us -> 64.9 us (1.066)
  the two profiles are of different devices: /device:TPU:21 before, /device:TPU:0 now
where the time goes in v2:
time: 64.9 us; the launch traced here: 64.6 us
  Pallas kernels  60.1 us (93%)
  local copies, waits for them, and re-layouts  4.41 us (7%)
    pallas_call x1, Pallas kernels, on_device(): pl.pallas_call(functools.partial(kernel, nz, nx, cap, parts), out_shape=j...  60.1 us
    unnamed x3, local copies, waits for them, and re-layouts  4.41 us

profile of v2, /device:TPU:0, one launch (start us, length us, event | category | flops | bytes accessed | tf_op | source)
XLA Modules:
  0.0 64.6 jit_solution(15298614115377523488)
XLA Ops:
  0.0 1.4 %copy.8.index_ref = s32[10,4]{1,0:T(8,128)} copy(s32[10,4]{0,1:T(4,128)} %param.10) | data formatting | bytes 320 | tf_op args[4]
  1.4 1.4 %copy.7.source_ref = s32[40,16]{1,0:T(8,128)} copy(s32[40,16]{0,1:T(8,128)} %param.9) | data formatting | bytes 5120 | tf_op args[3]
  2.7 60.1 %shard_map.64 = f32[4,64,256]{2,1,0:T(8,128)} custom-call(s32[40,16]{1,0:T(8,128)} %copy.7.source_ref, s32[10,4]{1,0:T(8,128)} %copy.8.index_ref, f32[24]{0:T(128)} %table_ref.1, f32[4,256,256]{2,1,0:T(8,128)} %psi_ref.1, f32[10,4,256,256]{3,2,1,0:T(8,128)} %left_ref.1, f32[10,4,256,256]{3,2,1,0:T(8,128)} %right_ref.1), custom_call_target="tpu_custom_call" | custom-call | flops 8053063680 | bytes 20971520 | tf_op jit(solution)/shard_map/pallas_call | solution.py:284
  62.9 1.7 %copy.10 = f32[4,64,256]{2,1,0:T(8,128)} copy(f32[4,64,256]{2,1,0:T(8,128)} %shard_map.64) | data formatting | bytes 524288

commit v3 on v2

--- a/solution.py
+++ b/solution.py
@@ -140,7 +140,7 @@
             v_hi, v_lo = split(value)
             contrib[k * cap + j] = dot3(l_hi, l_lo, v_hi, v_lo)
             return after[p]
-        return lax.fori_loop(begin, end, pair, start)
+        return lax.fori_loop(begin, end, pair, start, unroll=True)
 
     ready(z)
     head = chain(z)
@@ -189,12 +189,11 @@
         @pl.when(d == 1)
         def _():
             products(z, cap // 2, cap, middle)
+        for i in range(parts):
+            both(d - 1, take_x(i))
         both(d - 1, take_all)
-        for i in range(parts):
-            both(d, take_x(i))
-        return carry
-    lax.fori_loop(1, nz, stage, 0)
-    both(nz - 1, take_all)
+        return carry
+    lax.fori_loop(1, nz + 1, stage, 0)
 
     def mine(t, xq, core):
         return h.at[t, pl.ds(pl.multiple_of((2 * xq + core) * rows, rows), rows), :]

time: 64.9 us -> 51 us (0.79)
  Pallas kernels: 60.1 us -> 46.3 us
    pallas_call x1, Pallas kernels: 60.1 us -> 46.3 us  [on_device(): pl.pallas_call(functools.partial(kernel, nz, nx, cap, parts), out_shape=j...]
where the time goes in v3:
time: 51 us; the launch traced here: 50.7 us
  Pallas kernels  46.3 us (91%)
  local copies, waits for them, and re-layouts  4.41 us (9%)
    pallas_call x1, Pallas kernels, on_device(): pl.pallas_call(functools.partial(kernel, nz, nx, cap, parts), out_shape=j...  46.3 us
    unnamed x3, local copies, waits for them, and re-layouts  4.41 us

profile of v3, /device:TPU:0, one launch (start us, length us, event | category | flops | bytes accessed | tf_op | source)
XLA Modules:
  0.0 50.7 jit_solution(11865956180496757127)
XLA Ops:
  0.0 1.4 %copy.8.index_ref = s32[10,4]{1,0:T(8,128)} copy(s32[10,4]{0,1:T(4,128)} %param.10) | data formatting | bytes 320 | tf_op args[4]
  1.4 1.4 %copy.7.source_ref = s32[40,16]{1,0:T(8,128)} copy(s32[40,16]{0,1:T(8,128)} %param.9) | data formatting | bytes 5120 | tf_op args[3]
  2.7 46.3 %shard_map.64 = f32[4,64,256]{2,1,0:T(8,128)} custom-call(s32[40,16]{1,0:T(8,128)} %copy.7.source_ref, s32[10,4]{1,0:T(8,128)} %copy.8.index_ref, f32[24]{0:T(128)} %table_ref.1, f32[4,256,256]{2,1,0:T(8,128)} %psi_ref.1, f32[10,4,256,256]{3,2,1,0:T(8,128)} %left_ref.1, f32[10,4,256,256]{3,2,1,0:T(8,128)} %right_ref.1), custom_call_target="tpu_custom_call" | custom-call | flops 8053063680 | bytes 20971520 | tf_op jit(solution)/shard_map/pallas_call | solution.py:283
  49.1 1.7 %copy.10 = f32[4,64,256]{2,1,0:T(8,128)} copy(f32[4,64,256]{2,1,0:T(8,128)} %shard_map.64) | data formatting | bytes 524288

commit v4 on v3

--- a/solution.py
+++ b/solution.py
@@ -22,8 +22,8 @@
     return dot(a_hi, b_hi) + dot(a_hi, b_lo) + dot(a_lo, b_hi)
 
 
-def kernel(nz, nx, cap, parts, source_ref, index_ref, table_ref, psi_ref, left_ref, right_ref, out_ref,
-           after, rank, reads, psi_all, left, right, cur_hi, cur_lo, contrib, h, first, summed, second,
+def kernel(nz, nx, cap, parts, source_hbm, index_hbm, table_ref, psi_ref, left_ref, right_ref, out_ref,
+           source_ref, index_ref, after, rank, reads, middle, psi_all, left, right, cur_hi, cur_lo, contrib, h, first, summed, second,
            load_sem, recv_sem, z_sem, x_sem, c_sem, r1_send, r1_recv, r2_send, r2_recv):
     sec = psi_ref.shape[0]
     block = psi_ref.shape[1]
@@ -42,8 +42,10 @@
     load_right = pltpu.make_async_copy(right_ref, right, load_sem.at[1])
     load_left = pltpu.make_async_copy(left_ref, left, load_sem.at[2])
     load_psi.start()
-    load_right.start()
-    load_left.start()
+    load_source = pltpu.make_async_copy(source_hbm, source_ref, load_sem.at[3])
+    load_index = pltpu.make_async_copy(index_hbm, index_ref, load_sem.at[4])
+    load_source.start()
+    load_index.start()
 
     def other(step):
         return lax.rem(x + step, nx)
@@ -98,9 +100,14 @@
             @pl.when(jnp.logical_and(z + way >= 0, z + way < nz))
             def _():
                 z_copy(z, i, way).start()
+    load_right.start()
+    load_left.start()
 
     def source_of(p):
-        return source_ref[o * terms + lax.div(p, sec), z * sec + lax.rem(p, sec)]
+        return source_ref[z * sec + lax.rem(p, sec), o * terms + lax.div(p, sec)]
+
+    load_source.wait()
+    load_index.wait()
 
     def clear(p, carry):
         rank[p] = 0
@@ -135,7 +142,7 @@
             t = lax.rem(p, sec)
             s = lax.rem(source_of(p), sec)
             r_hi, r_lo = split(right[w, t])
-            value = dot3(cur_hi[s], cur_lo[s], r_hi, r_lo) * table_ref[index_ref[w, t]]
+            value = dot3(cur_hi[s], cur_lo[s], r_hi, r_lo) * table_ref[index_ref[t, w]]
             l_hi, l_lo = split(left[w, t])
             v_hi, v_lo = split(value)
             contrib[k * cap + j] = dot3(l_hi, l_lo, v_hi, v_lo)
@@ -144,10 +151,6 @@
 
     ready(z)
     head = chain(z)
-    load_right.wait()
-    load_left.wait()
-    middle = products(z, 0, cap // 2, head)
-
     def both(d, body):
         for side in (-1, 1):
             k = z + side * d
@@ -176,11 +179,12 @@
         return body
 
     def take_all(k, side):
+        start = chain(k)
         for i in range(parts):
             for xq in range(nx):
                 arrived(k, i, 2 * xq + 1 - c)
         ready(k)
-        products(k, 0, cap, chain(k))
+        products(k, 0, cap, start)
 
     def stage(d, carry):
         for i in range(parts):
@@ -188,7 +192,13 @@
 
         @pl.when(d == 1)
         def _():
-            products(z, cap // 2, cap, middle)
+            load_right.wait()
+            load_left.wait()
+            middle[0] = products(z, 0, cap // 2, head)
+
+        @pl.when(d == 2)
+        def _():
+            products(z, cap // 2, cap, middle[0])
         for i in range(parts):
             both(d - 1, take_x(i))
         both(d - 1, take_all)
@@ -276,19 +286,22 @@
     slots = cap * nz
     nx = nop // 2
     rows = block // nop
-    parts = 2
+    parts = 1
     dma = pltpu.SemaphoreType.DMA
     smem = pl.BlockSpec(memory_space=pltpu.SMEM)
     hbm = pl.BlockSpec(memory_space=pl.ANY)
     return pl.pallas_call(
         functools.partial(kernel, nz, nx, cap, parts),
         out_shape=jax.ShapeDtypeStruct((sec, rows, block), F32),
-        in_specs=[smem] * 3 + [hbm] * 3,
+        in_specs=[hbm] * 2 + [smem] + [hbm] * 3,
         out_specs=pl.BlockSpec(memory_space=pltpu.VMEM),
         scratch_shapes=[
+            pltpu.SMEM(source.shape[::-1], jnp.int32),
+            pltpu.SMEM(coef_index.shape[::-1], jnp.int32),
             pltpu.SMEM((pairs,), jnp.int32),
             pltpu.SMEM((pairs,), jnp.int32),
             pltpu.SMEM((nz,), jnp.int32),
+            pltpu.SMEM((1,), jnp.int32),
             pltpu.VMEM((nz, sec, block, block), F32),
             pltpu.VMEM((terms, sec, block, block), F32),
             pltpu.VMEM((terms, sec, block, block), F32),
@@ -299,7 +312,7 @@
             pltpu.VMEM((sec, nx, rows, block), F32),
             pltpu.VMEM((sec, nx, rows, block), F32),
             pltpu.VMEM((sec, nx, rows, block), F32),
-            dma((3,)),
+            dma((5,)),
             dma((nz, parts, nop)),
             dma((2, nz, parts)),
             dma((nz, parts, nx)),
@@ -315,7 +328,7 @@
         cost_estimate=pl.CostEstimate(
             flops=12 * pairs * block ** 3, bytes_accessed=8 * pairs * block * block, transcendentals=0
         ),
-    )(source, coef_index, coef_table, psi, left_env, right_env)
+    )(source.T, coef_index.T, coef_table, psi, left_env, right_env)
 
 
 def solution(mesh):

time: 51 us -> 47 us (0.922)
  local copies, waits for them, and re-layouts: 4.41 us -> 1.67 us
  Pallas kernels: 46.3 us -> 45.2 us
    unnamed x3 -> x1, local copies, waits for them, and re-layouts: 4.41 us -> 1.67 us
    pallas_call x1, Pallas kernels: 46.3 us -> 45.2 us  [on_device(): pl.pallas_call(functools.partial(kernel, nz, nx, cap, parts), out_shape=j...]
where the time goes in v4:
time: 47 us; the launch traced here: 46.8 us
  Pallas kernels  45.2 us (96%)
  local copies, waits for them, and re-layouts  1.67 us (4%)
    pallas_call x1, Pallas kernels, on_device(): pl.pallas_call(functools.partial(kernel, nz, nx, cap, parts), out_shape=j...  45.2 us
    unnamed x1, local copies, waits for them, and re-layouts  1.67 us

profile of v4, /device:TPU:0, one launch (start us, length us, event | category | flops | bytes accessed | tf_op | source)
XLA Modules:
  0.0 46.8 jit_solution(15394523380826158868)
XLA Ops:
  0.0 45.2 %shard_map.64 = f32[4,64,256]{2,1,0:T(8,128)} custom-call(s32[16,40]{1,0:T(8,128)} %bitcast.2, s32[4,10]{1,0:T(4,128)} %bitcast.3, f32[24]{0:T(128)} %table_ref.1, f32[4,256,256]{2,1,0:T(8,128)} %psi_ref.1, f32[10,4,256,256]{3,2,1,0:T(8,128)} %left_ref.1, f32[10,4,256,256]{3,2,1,0:T(8,128)} %right_ref.1), custom_call_target="tpu_custom_call" | custom-call | flops 8053063680 | bytes 20971520 | tf_op jit(solution)/shard_map/pallas_call | solution.py:293
  45.2 1.7 %copy.8 = f32[4,64,256]{2,1,0:T(8,128)} copy(f32[4,64,256]{2,1,0:T(8,128)} %shard_map.64) | data formatting | bytes 524288

commit v5 on v4

--- a/solution.py
+++ b/solution.py
@@ -122,7 +122,7 @@
             after[p] = found
             rank[p] = jnp.where(hit, count, rank[p])
             return jnp.where(hit, p, found), jnp.where(hit, count + 1, count)
-        found, count = lax.fori_loop(0, pairs, backward, (0, 0))
+        found, count = lax.fori_loop(0, pairs, backward, (0, 0), unroll=True)
         reads[k] = count
         return found
 
@@ -134,7 +134,7 @@
         def halve(s, carry):
             cur_hi[s], cur_lo[s] = split(psi_all[k, s])
             return carry
-        lax.fori_loop(0, sec, halve, 0)
+        lax.fori_loop(0, sec, halve, 0, unroll=True)
 
     def products(k, begin, end, start):
         def pair(j, p):
@@ -196,11 +196,12 @@
             load_left.wait()
             middle[0] = products(z, 0, cap // 2, head)
 
+        for i in range(parts):
+            both(d - 1, take_x(i))
+
         @pl.when(d == 2)
         def _():
             products(z, cap // 2, cap, middle[0])
-        for i in range(parts):
-            both(d - 1, take_x(i))
         both(d - 1, take_all)
         return carry
     lax.fori_loop(1, nz + 1, stage, 0)
@@ -221,12 +222,19 @@
     def target(t, carry):
         @pl.when(t < sec)
         def _():
-            total = contrib[slot(t)]
-            for w in range(1, terms):
-                total = total + contrib[slot(w * sec + t)]
-            h[t] = total
-            for xq in range(nx):
+            at = [slot(w * sec + t) for w in range(terms)]
+
+            def gather(xq, core):
+                own = pl.ds(pl.multiple_of((2 * xq + core) * rows, rows), rows)
+                total = contrib[at[0], own, :]
+                for w in range(1, terms):
+                    total = total + contrib[at[w], own, :]
+                h[t, own, :] = total
+            for xq in range(nx):
+                gather(xq, 1 - c)
                 r1_copy(t, xq).start()
+            for xq in range(nx):
+                gather(xq, c)
 
         @pl.when(t >= 1)
         def _():

time: 47 us -> 46.2 us (0.983)
  Pallas kernels: 45.2 us -> 44.4 us
    pallas_call x1, Pallas kernels: 45.2 us -> 44.4 us  [on_device(): pl.pallas_call(functools.partial(kernel, nz, nx, cap, parts), out_shape=j...]
where the time goes in v5:
time: 46.2 us; the launch traced here: 46 us
  Pallas kernels  44.4 us (96%)
  local copies, waits for them, and re-layouts  1.67 us (4%)
    pallas_call x1, Pallas kernels, on_device(): pl.pallas_call(functools.partial(kernel, nz, nx, cap, parts), out_shape=j...  44.4 us
    unnamed x1, local copies, waits for them, and re-layouts  1.67 us

profile of v5, /device:TPU:0, one launch (start us, length us, event | category | flops | bytes accessed | tf_op | source)
XLA Modules:
  0.0 46.0 jit_solution(3352661910827521412)
XLA Ops:
  0.0 44.4 %shard_map.64 = f32[4,64,256]{2,1,0:T(8,128)} custom-call(s32[16,40]{1,0:T(8,128)} %bitcast.2, s32[4,10]{1,0:T(4,128)} %bitcast.3, f32[24]{0:T(128)} %table_ref.1, f32[4,256,256]{2,1,0:T(8,128)} %psi_ref.1, f32[10,4,256,256]{3,2,1,0:T(8,128)} %left_ref.1, f32[10,4,256,256]{3,2,1,0:T(8,128)} %right_ref.1), custom_call_target="tpu_custom_call" | custom-call | flops 8053063680 | bytes 20971520 | tf_op jit(solution)/shard_map/pallas_call | solution.py:301
  44.4 1.7 %copy.8 = f32[4,64,256]{2,1,0:T(8,128)} copy(f32[4,64,256]{2,1,0:T(8,128)} %shard_map.64) | data formatting | bytes 524288
